TPU v7x, 256 devices: a whole 4x4x8 slice. The times are simulated.
256 devices in a mesh: gx: 4 (over x_lo, core), gy: 8 (over z), gz: 8 (over y, x_hi).
Axes of the slice: x: 4 (x_hi: 2, x_lo: 2; x = x_hi * 2 + x_lo), y: 4, z: 8, core: 2. Of those that a mesh axis runs over, the one named last changes fastest.
Arguments:
- charges: float32 [4, 8, 8, 1024], P('gx', 'gy', 'gz'), may hold values from -6 to 6
- cells: int32 [4, 8, 8, 3, 1024], P('gx', 'gy', 'gz'), may hold values from 0 to 391, as said below
- counts: int32 [4, 8, 8], P('gx', 'gy', 'gz'), may hold values from 128 to 1024, as said below
Outputs:
- potential: float32 [128, 256, 3072], P('gx', 'gy', 'gz')
- forces: float32 [4, 8, 8, 3, 1024], P('gx', 'gy', 'gz')
Inputs may be any that keep to these rules, and one draw needn't show every extreme that they name: `cells`: component 0 lies below 40, component 1 below 40, component 2 below 392. Slots at or past a brick's count are unused. `counts`: some brick holds 1024 atoms.
All inputs are finite; a program needn't handle non-finite values.
Results may differ from a plain program's by a relative error of at most 0.0075.
Values sent between devices are 32-bit elements; how exact they have to be, the bound alone decides.
No kernel may reach another device: no remote copies, remote signals or barrier semaphores. Data moves between devices by JAX's collectives and lax.ppermute only.
A program may use at most 128 MiB of HBM per device.

v0:
```python
import functools
import math

import jax
import jax.numpy as jnp
from jax import lax
from jax.experimental import pallas as pl
from jax.experimental.pallas import tpu as pltpu
from jax.sharding import PartitionSpec as P

BX = 32
BY = 32
BZ = 384
A_DEV = 1024
PAD = 4
REACH = 4
WIDTH = A_DEV + 128
BLOCK = 256
WIDE = 2 * BLOCK

X0 = 5
Y0 = 8
PX = 42
PY = 48
PZ = 512
CHUNK = 14
FX = 40
FY = 40
FCHUNK = 20

kernel_width = 2.0
EXPONENT = -math.log2(math.e) / (2.0 * kernel_width * kernel_width)
SCALE = 1.3903614627339054
UNIT = math.sqrt(-EXPONENT)
LOW_END = 2 * PAD + 5
HIGH_START = BZ + PAD - 9
SPAN = A_DEV + 128 + WIDE
MERGED = 9 * A_DEV + SPAN
ROWS = FCHUNK * FY


def weight(first, second, scale=1.0):
    away = first - second
    square = away * away
    value = jnp.exp2(math.log2(scale) - square)
    return jnp.where(square < (REACH + 0.5) ** 2 * UNIT * UNIT, value, 0.0)


def iota(shape, dim):
    return lax.broadcasted_iota(jnp.int32, shape, dim).astype(jnp.float32)


def toward(axis):
    return 1 - 2 * (lax.axis_index(axis) % 2)


def compact(numbers, charges, cells, own, first, second, lists):
    count = numbers[0]
    slots = lax.broadcasted_iota(jnp.int32, (1, A_DEV), 1)
    live = slots < count
    charge = jnp.where(live, charges[...], 0.0).astype(jnp.bfloat16).astype(jnp.float32)
    places = jnp.concatenate([jnp.where(live, cells[i], 0) for i in range(3)], axis=0)
    own[0:1, 0:A_DEV] = charge
    own[1:4, 0:A_DEV] = places.astype(jnp.float32)
    own[:, A_DEV:WIDTH] = jnp.full((4, WIDTH - A_DEV), count.astype(jnp.float32))
    depth = places[2:3]
    before = jnp.concatenate(
        [
            jnp.where(live & (depth < LOW_END), 1.0, 0.0),
            jnp.where(live & (depth >= HIGH_START), 1.0, 0.0),
            jnp.zeros((6, A_DEV), jnp.float32),
        ],
        axis=0,
    )
    near = before
    lanes = lax.broadcasted_iota(jnp.int32, (8, A_DEV), 1)
    shift = 1
    while shift < A_DEV:
        before = before + jnp.where(lanes >= shift, pltpu.roll(before, shift, 1), 0.0)
        shift *= 2
    totals = before[:, A_DEV - 1 : A_DEV]
    spot = jnp.where(near > 0.5, before - 1.0, -1.0)
    steps = (jnp.max(totals).astype(jnp.int32) + BLOCK - 1) // BLOCK
    for side in range(2):
        lists[side, :, 0:A_DEV] = jnp.zeros((4, A_DEV), jnp.float32)
        lists[side, :, A_DEV:WIDTH] = jnp.broadcast_to(
            totals[side : side + 1], (4, WIDTH - A_DEV)
        )

    def window(k, _):
        for side, base in enumerate((0, BZ // 2)):
            rows = jnp.concatenate(
                [
                    charge,
                    places[0:2].astype(jnp.float32),
                    (places[2:3] - base).astype(jnp.float32),
                    jnp.zeros((4, A_DEV), jnp.float32),
                ],
                axis=0,
            ).astype(jnp.bfloat16)
            want = iota((BLOCK, A_DEV), 0) + (k * BLOCK).astype(jnp.float32)
            pick = jnp.where(want == spot[side : side + 1], 1.0, 0.0).astype(jnp.bfloat16)
            moved = lax.dot_general(
                rows, pick, (((1,), (1,)), ((), ())), preferred_element_type=jnp.float32
            )
            cols = pl.ds(pl.multiple_of(k * BLOCK, BLOCK), BLOCK)
            lists[side, 0:3, cols] = moved[0:3]
            lists[side, 3:4, cols] = moved[3:4] + float(base)
        return 0

    lax.fori_loop(0, steps, window, 0)
    odd = lax.axis_index("gz") % 2
    first[...] = lists[1 - odd]
    second[...] = lists[odd]


def append(ref, brick, number, offset, dx, dy, dz, merged):
    lanes = lax.broadcasted_iota(jnp.int32, (1, A_DEV), 1)
    live = lanes < number
    moved = (X0 - PAD + BX * dx, Y0 - PAD + BY * dy, BZ * dz - PAD)
    rows = [ref[brick, 0:1, 0:A_DEV]]
    for i in range(3):
        place = ref[brick, 1 + i : 2 + i, 0:A_DEV] + jnp.float32(moved[i])
        rows.append(jnp.where(live, place * UNIT, 0.0))
    atoms = jnp.concatenate(rows + [jnp.zeros((4, A_DEV), jnp.float32)], axis=0)
    atoms = jnp.concatenate([atoms, jnp.zeros((8, SPAN - A_DEV), jnp.float32)], axis=1)
    atoms = pltpu.roll(atoms, offset % 128, 1)
    start = pl.multiple_of(offset // 128 * 128, 128)
    merged[:, pl.ds(start, 128)] += atoms[:, 0:128]
    merged[:, pl.ds(start + 128, SPAN - 128)] = atoms[:, 128:SPAN]
    return offset + number


def spread(merged, start, size, x0, nx, y0, ny, grid, rows_x, first):
    cols = pl.ds(pl.multiple_of(start, BLOCK), size)
    charge = merged[0:1, cols]
    xa = merged[1:2, cols]
    ya = merged[2:3, cols]
    za = merged[3:4, cols]
    gy = weight((iota((ny, size), 0) + jnp.float32(y0)) * UNIT, ya) * (charge * (1.0 / SCALE))
    zi = iota((PZ, size), 0)
    zi = jnp.where(zi < 448.0, zi, zi - float(PZ)) * UNIT
    right = weight(zi, za, SCALE).astype(jnp.bfloat16)
    rows_x[:, 0:size] = weight(iota((48, size), 0) * UNIT, xa)
    chunk = min(nx, CHUNK * PY // ny)
    for c in range(0, nx, chunk):
        at = x0 + c
        left = jnp.stack(
            [rows_x[pl.ds(at + i, 1), 0:size] * gy for i in range(chunk)], axis=0
        )
        left = left.reshape(chunk * ny, size).astype(jnp.bfloat16)
        part = lax.dot_general(
            left, right, (((1,), (1,)), ((), ())), preferred_element_type=jnp.float32
        )
        part = part.reshape(chunk, ny, PZ)
        if first:
            grid[pl.ds(at, chunk), pl.ds(y0, ny), :] = part
        else:
            grid[pl.ds(at, chunk), pl.ds(y0, ny), :] += part


def spread_all(merged, total, x0, nx, y0, ny, grid, rows_x, clear):
    rest = total % WIDE
    wide = total // WIDE + (rest > BLOCK).astype(jnp.int32)
    if clear:
        wide = jnp.maximum(wide, 1)
        spread(merged, 0, WIDE, x0, nx, y0, ny, grid, rows_x, True)

    def block(k, _):
        spread(merged, k * WIDE, WIDE, x0, nx, y0, ny, grid, rows_x, False)
        return 0

    lax.fori_loop(1 if clear else 0, wide, block, 0)

    @pl.when(total > wide * WIDE)
    def _():
        spread(merged, wide * WIDE, BLOCK, x0, nx, y0, ny, grid, rows_x, False)


def gather(ref, bricks, numbers, merged):
    merged[:, 0:128] = jnp.zeros((8, 128), jnp.float32)
    offset = jnp.int32(0)
    for brick, (dx, dy, dz) in bricks:
        number = numbers[brick, 0, 0].astype(jnp.int32)
        offset = append(ref, brick, number, offset, dx, dy, dz, merged)
    return offset


def slots_of(axis):
    step = toward(axis)
    return (step, 0, -step)


def column(lists, grid, rows_x, merged, numbers, sem):
    copy = pltpu.make_async_copy(lists.at[:, 0:1, A_DEV:WIDTH], numbers, sem)
    copy.start()
    copy.wait()
    xs, zs = slots_of("gx"), slots_of("gz")
    for i in (1, 0, 2):
        total = gather(
            lists,
            [(3 * i + j, (xs[i], 0, zs[j])) for j in (1, 0, 2)],
            numbers,
            merged,
        )
        if i == 1:
            spread_all(merged, total, 0, PX, 0, PY, grid, rows_x, True)
        else:
            x0 = jnp.where(xs[i] > 0, 28, 0)
            spread_all(merged, total, x0, 14, 0, PY, grid, rows_x, False)


def finish(
    near, far, own, charges, before, potential, forces, grid,
    rows_x, fields, merged, numbers, charge, sems,
):
    copies = [
        pltpu.make_async_copy(near.at[:, 0:1, A_DEV:WIDTH], numbers.at[0], sems.at[0]),
        pltpu.make_async_copy(far.at[:, 0:1, A_DEV:WIDTH], numbers.at[1], sems.at[1]),
        pltpu.make_async_copy(own.at[:, 0:1, A_DEV:WIDTH], numbers.at[2, 0:1], sems.at[2]),
        pltpu.make_async_copy(charges, charge, sems.at[3]),
    ]
    for copy in copies:
        copy.start()
    for copy in copies:
        copy.wait()
    xs, zs = slots_of("gx"), slots_of("gz")
    dy = toward("gy")
    for i, ref in enumerate((near, far)):
        step = dy * (1 - 2 * i)
        total = gather(
            ref,
            [(3 * m + j, (xs[m], step, zs[j])) for m in range(3) for j in range(3)],
            numbers.at[i],
            merged,
        )
        y0 = pl.multiple_of(jnp.where(step > 0, 32, 0), 8)
        spread_all(merged, total, 0, PX, y0, 16, grid, rows_x, False)
    copy = pltpu.make_async_copy(
        grid.at[X0 : X0 + BX, Y0 : Y0 + BY, 0:BZ], potential, sems.at[0]
    )
    copy.start()

    forces[...] = jnp.zeros_like(forces)
    count = numbers[2, 0, 0, 0].astype(jnp.int32)

    def build(c):
        gx, gy, gz = [], [], []
        for x in range(c * FCHUNK, (c + 1) * FCHUNK):
            gx.append(grid[x + 2, 4:44, :] - grid[x, 4:44, :])
            gy.append(grid[x + 1, 5:45, :] - grid[x + 1, 3:43, :])
            mid = grid[x + 1, 4:44, :]
            gz.append(pltpu.roll(mid, PZ - 2, 1) - mid)
        for d, parts in enumerate((gx, gy, gz)):
            both = jnp.stack(parts, axis=0).reshape(ROWS, PZ).astype(jnp.bfloat16)
            fields[d, c * ROWS : (c + 1) * ROWS, :] = both

    def sample(start, size, fresh):
        cols = pl.ds(pl.multiple_of(start, BLOCK), size)
        xa = own[0, 1:2, cols]
        za = own[0, 3:4, cols] - float(PAD)
        zi = iota((PZ, size), 0)
        zi = jnp.where(zi < 448.0, zi, zi - float(PZ))
        depth = jnp.where(zi == za, 1.0, 0.0).astype(jnp.bfloat16)
        below = jnp.where(zi == za - 1.0, 1.0, 0.0).astype(jnp.bfloat16)
        sums = [jnp.zeros((FY, size), jnp.float32)] * 3
        for c in range(FX // FCHUNK):
            if fresh:
                build(c)
            for d in range(3):
                part = jnp.dot(
                    fields[d, c * ROWS : (c + 1) * ROWS, :],
                    below if d == 2 else depth,
                    preferred_element_type=jnp.float32,
                ).reshape(FCHUNK, FY, size)
                for i in range(FCHUNK):
                    hot_x = xa == float(c * FCHUNK + i)
                    sums[d] = sums[d] + jnp.where(hot_x, part[i], 0.0)
        hot_y = iota((FY, size), 0) == own[0, 2:3, cols]
        slots = lax.broadcasted_iota(jnp.int32, (1, size), 1) + start
        factor = jnp.where(slots < count, -0.5 * charge[0:1, cols], 0.0)
        for d in range(3):
            value = jnp.sum(jnp.where(hot_y, sums[d], 0.0), axis=0, keepdims=True)
            forces[d, :, cols] = value * factor

    sample(0, WIDE, True)

    def more(k, _):
        sample(k * WIDE, WIDE, False)
        return 0

    lax.fori_loop(1, (count + WIDE - 1) // WIDE, more, 0)
    copy.wait()


def swaps(block, other, axis):
    size = lax.axis_size(axis)
    first = [(i, i ^ 1) for i in range(size)]
    second = [(i, (i + 1 if i % 2 else i - 1) % size) for i in range(size)]
    return lax.ppermute(block, axis, first), lax.ppermute(other, axis, second)


VMEM = pl.BlockSpec(memory_space=pltpu.VMEM)
HBM = pl.BlockSpec(memory_space=pl.ANY)
LIMIT = 40 * 1024 * 1024


def call_compact(counts, charge, cells):
    shape = pltpu.VMEM((4, WIDTH), jnp.float32)
    return pl.pallas_call(
        compact,
        out_shape=(shape, shape, shape),
        in_specs=[pl.BlockSpec(memory_space=pltpu.SMEM), VMEM, VMEM],
        out_specs=(VMEM,) * 3,
        scratch_shapes=[pltpu.VMEM((2, 4, WIDTH), jnp.float32)],
    )(counts, charge, cells)


def call_column(atoms):
    return pl.pallas_call(
        column,
        out_shape=pltpu.VMEM((PX, PY, PZ), jnp.float32),
        in_specs=[VMEM],
        out_specs=VMEM,
        scratch_shapes=[
            pltpu.VMEM((48, WIDE), jnp.float32),
            pltpu.VMEM((8, MERGED), jnp.float32),
            pltpu.SMEM((9, 1, WIDTH - A_DEV), jnp.float32),
            pltpu.SemaphoreType.DMA,
        ],
        compiler_params=pltpu.CompilerParams(vmem_limit_bytes=LIMIT),
        cost_estimate=pl.CostEstimate(flops=6 * 10**9, bytes_accessed=10**6, transcendentals=0),
    )(atoms)


def call_finish(near, far, own, charge, grid):
    potential, forces, _ = pl.pallas_call(
        finish,
        out_shape=(
            jax.ShapeDtypeStruct((BX, BY, BZ), jnp.float32),
            jax.ShapeDtypeStruct((3, 1, A_DEV), jnp.float32),
            pltpu.VMEM((PX, PY, PZ), jnp.float32),
        ),
        in_specs=[VMEM, VMEM, VMEM, HBM, VMEM],
        out_specs=(HBM, VMEM, VMEM),
        input_output_aliases={4: 2},
        scratch_shapes=[
            pltpu.VMEM((48, WIDE), jnp.float32),
            pltpu.VMEM((3, FX * FY, PZ), jnp.bfloat16),
            pltpu.VMEM((8, MERGED), jnp.float32),
            pltpu.SMEM((3, 9, 1, WIDTH - A_DEV), jnp.float32),
            pltpu.VMEM((1, A_DEV), jnp.float32),
            pltpu.SemaphoreType.DMA((4,)),
        ],
        compiler_params=pltpu.CompilerParams(vmem_limit_bytes=LIMIT),
    )(near, far, own, charge, grid)
    return potential, forces


def local(charges, cells, counts):
    charge = charges.reshape(1, A_DEV)
    own, first, second = call_compact(counts.reshape(1), charge, cells.reshape(3, 1, A_DEV))
    own = own[None]
    first, second = swaps(first[None], second[None], "gz")
    atoms = jnp.concatenate([first, own, second], axis=0)
    first, second = swaps(atoms, atoms, "gx")
    atoms = jnp.concatenate([first, atoms, second], axis=0)
    first, second = swaps(atoms, atoms, "gy")
    grid = call_column(atoms)
    potential, forces = call_finish(first, second, own, charge, grid)
    return potential, forces.reshape(1, 1, 1, 3, A_DEV)


def solution(mesh):
    in_specs = (P("gx", "gy", "gz", None), P("gx", "gy", "gz", None, None), P("gx", "gy", "gz"))
    out_specs = (P("gx", "gy", "gz"), P("gx", "gy", "gz", None, None))
    return jax.shard_map(local, mesh=mesh, in_specs=in_specs, out_specs=out_specs, check_vma=False)
```

profile of v0, /device:TPU:1, one launch (start us, length us, event | category | flops | bytes accessed | tf_op | source)
XLA Modules:
  0.0 38.9 jit_solution(4891949802261100927)
XLA Ops:
  1.3 1.8 %shard_map.50 = (f32[4,1152]{1,0:T(4,128)S(1)}, f32[4,1152]{1,0:T(4,128)S(1)}, f32[4,1152]{1,0:T(4,128)S(1)}) custom-call(s32[1]{0:T(128)} %bitcast.10.numbers, f32[1,1024]{1,0:T(1,128)} %bitcast.13, s32[3,1,1024]{2,1,0:T(1,128)} %bitcast.17), custom_call_target="tpu_custom_call" | custom-call | tf_op jit(solution)/shard_map/pallas_call | solution.py:310
  3.1 6.1 %collective-permute-start.1 = (f32[1,4,1152]{2,1,0:T(4,128)S(1)}, f32[1,4,1152]{2,1,0:T(4,128)S(1)}, u32[]{:S(2)}, u32[]{:S(2)}) collective-permute-start(f32[1,4,1152]{2,1,0:T(4,128)S(1)} %bitcast.16), channel_id=1, source_target_pairs={{0,7},{1,2},{2,1},{3,4},{4,3},{5,6},{6,5},{7,0},{8,15},{9,10},{10,... | collective-permute-start | bytes 55304 | tf_op jit(solution)/shard_map/ppermute | solution.py:300
  9.2 0.0 collective-permute-start
  9.2 1.1 %collective-permute-done.1 = f32[1,4,1152]{2,1,0:T(4,128)S(1)} collective-permute-done((f32[1,4,1152]{2,1,0:T(4,128)S(1)}, f32[1,4,1152]{2,1,0:T(4,128)S(1)}, u32[]{:S(2)}, u32[]{:S(2)}) %collective-permute-start.1) | collective-permute-done | bytes 18464 | tf_op jit(solution)/shard_map/ppermute | solution.py:300
  10.3 3.0 %collective-permute-done = f32[1,4,1152]{2,1,0:T(4,128)S(1)} collective-permute-done((f32[1,4,1152]{2,1,0:T(4,128)S(1)}, f32[1,4,1152]{2,1,0:T(4,128)S(1)}, u32[]{:S(2)}, u32[]{:S(2)}) %collective-permute-start) | collective-permute-done | bytes 18464 | tf_op jit(solution)/shard_map/ppermute | solution.py:300
  13.4 2.1 %collective-permute-start.2 = (f32[3,4,1152]{2,1,0:T(4,128)S(1)}, f32[3,4,1152]{2,1,0:T(4,128)S(1)}, u32[]{:S(2)}, u32[]{:S(2)}) collective-permute-start(f32[3,4,1152]{2,1,0:T(4,128)S(1)} %pad_maximum_fusion), channel_id=1, source_target_pairs={{0,64},{64,0},{128,192},{192,128},{1,65},{65,1},{129,193},{193,129... | collective-permute-start | bytes 165896 | tf_op jit(solution)/shard_map/ppermute | solution.py:300
  15.5 0.3 collective-permute-start.3
  15.8 0.6 %collective-permute-done.2 = f32[3,4,1152]{2,1,0:T(4,128)S(1)} collective-permute-done((f32[3,4,1152]{2,1,0:T(4,128)S(1)}, f32[3,4,1152]{2,1,0:T(4,128)S(1)}, u32[]{:S(2)}, u32[]{:S(2)}) %collective-permute-start.2) | collective-permute-done | bytes 55328 | tf_op jit(solution)/shard_map/ppermute | solution.py:300
  16.4 2.7 %collective-permute-done.3 = f32[3,4,1152]{2,1,0:T(4,128)S(1)} collective-permute-done((f32[3,4,1152]{2,1,0:T(4,128)S(1)}, f32[3,4,1152]{2,1,0:T(4,128)S(1)}, u32[]{:S(2)}, u32[]{:S(2)}) %collective-permute-start.3) | collective-permute-done | bytes 55328 | tf_op jit(solution)/shard_map/ppermute | solution.py:300
  19.1 0.0 copy-start
  19.1 5.7 %collective-permute-start.5 = (f32[9,4,1152]{2,1,0:T(4,128)S(1)}, f32[9,4,1152]{2,1,0:T(4,128)S(1)}, u32[]{:S(2)}, u32[]{:S(2)}) collective-permute-start(f32[9,4,1152]{2,1,0:T(4,128)S(1)} %constant_dynamic-update-slice_fusion.lists), channel_id=1, source_target_pairs={{0,56},{8,16},{16,8},{24,32},{32,24},{40,48},{48,40},{56,0},{1,57}... | collective-permute-start | bytes 497672 | tf_op jit(solution)/shard_map/ppermute | solution.py:300
  24.8 0.0 collective-permute-start.4
  24.8 3.7 %shard_map.51.before = f32[42,48,512]{2,1,0:T(8,128)S(1)} custom-call(f32[9,4,1152]{2,1,0:T(4,128)S(1)} %constant_dynamic-update-slice_fusion.lists), custom_call_target="tpu_custom_call" | custom-call | flops 6000000000 | bytes 1000000 | tf_op jit(solution)/shard_map/pallas_call | solution.py:320
  28.6 0.8 %collective-permute-done.5.far = f32[9,4,1152]{2,1,0:T(4,128)S(1)} collective-permute-done((f32[9,4,1152]{2,1,0:T(4,128)S(1)}, f32[9,4,1152]{2,1,0:T(4,128)S(1)}, u32[]{:S(2)}, u32[]{:S(2)}) %collective-permute-start.5) | collective-permute-done | bytes 165920 | tf_op jit(solution)/shard_map/ppermute | solution.py:300
  29.3 1.0 %collective-permute-done.4.near = f32[9,4,1152]{2,1,0:T(4,128)S(1)} collective-permute-done((f32[9,4,1152]{2,1,0:T(4,128)S(1)}, f32[9,4,1152]{2,1,0:T(4,128)S(1)}, u32[]{:S(2)}, u32[]{:S(2)}) %collective-permute-start.4) | collective-permute-done | bytes 165920 | tf_op jit(solution)/shard_map/ppermute | solution.py:300
  30.3 0.0 copy-done
  30.3 8.5 %shard_map.52 = (f32[32,32,384]{2,1,0:T(8,128)}, f32[3,1,1024]{2,1,0:T(1,128)}, f32[42,48,512]{2,1,0:T(8,128)S(1)}) custom-call(f32[9,4,1152]{2,1,0:T(4,128)S(1)} %collective-permute-done.4.near, f32[9,4,1152]{2,1,0:T(4,128)S(1)} %collective-permute-done.5.far, f32[1,4,1152]{2,1,0:T(4,128)S(1)} %bitcast.12, ...), custom_call_target="tpu_custom_call", output_to_operand_aliasing={{2}: (4, {})} | custom-call | tf_op jit(solution)/shard_map/pallas_call | solution.py:337
  (6 shorter events, 0.1 us)
Async XLA Ops:
  3.1 7.3 %collective-permute-start.1 = (f32[1,4,1152]{2,1,0:T(4,128)S(1)}, f32[1,4,1152]{2,1,0:T(4,128)S(1)}, u32[]{:S(2)}, u32[]{:S(2)}) collective-permute-start(f32[1,4,1152]{2,1,0:T(4,128)S(1)} %bitcast.16), channel_id=1, source_target_pairs={{0,7},{1,2},{2,1},{3,4},{4,3},{5,6},{6,5},{7,0},{8,15},{9,10},{10,... | collective-permute-start | bytes 55304 | tf_op jit(solution)/shard_map/ppermute | solution.py:300
  9.2 4.2 %collective-permute-start = (f32[1,4,1152]{2,1,0:T(4,128)S(1)}, f32[1,4,1152]{2,1,0:T(4,128)S(1)}, u32[]{:S(2)}, u32[]{:S(2)}) collective-permute-start(f32[1,4,1152]{2,1,0:T(4,128)S(1)} %bitcast.15), channel_id=1, source_target_pairs={{0,1},{1,0},{2,3},{3,2},{4,5},{5,4},{6,7},{7,6},{8,9},{9,8},{10,11... | collective-permute-start | bytes 55304 | tf_op jit(solution)/shard_map/ppermute | solution.py:300
  13.4 3.0 %collective-permute-start.2 = (f32[3,4,1152]{2,1,0:T(4,128)S(1)}, f32[3,4,1152]{2,1,0:T(4,128)S(1)}, u32[]{:S(2)}, u32[]{:S(2)}) collective-permute-start(f32[3,4,1152]{2,1,0:T(4,128)S(1)} %pad_maximum_fusion), channel_id=1, source_target_pairs={{0,64},{64,0},{128,192},{192,128},{1,65},{65,1},{129,193},{193,129... | collective-permute-start | bytes 165896 | tf_op jit(solution)/shard_map/ppermute | solution.py:300
  15.5 3.6 %collective-permute-start.3 = (f32[3,4,1152]{2,1,0:T(4,128)S(1)}, f32[3,4,1152]{2,1,0:T(4,128)S(1)}, u32[]{:S(2)}, u32[]{:S(2)}) collective-permute-start(f32[3,4,1152]{2,1,0:T(4,128)S(1)} %pad_maximum_fusion), channel_id=1, source_target_pairs={{0,192},{64,128},{128,64},{192,0},{1,193},{65,129},{129,65},{193,1... | collective-permute-start | bytes 165896 | tf_op jit(solution)/shard_map/ppermute | solution.py:300
  19.1 11.2 %copy-start = (f32[1,1,1,1024]{3,2,1,0:T(1,128)S(1)}, f32[1,1,1,1024]{3,2,1,0:T(1,128)}, u32[]{:S(2)}) copy-start(f32[1,1,1,1024]{3,2,1,0:T(1,128)} %param.3) | copy-start | bytes 12292
  19.1 10.2 %collective-permute-start.5 = (f32[9,4,1152]{2,1,0:T(4,128)S(1)}, f32[9,4,1152]{2,1,0:T(4,128)S(1)}, u32[]{:S(2)}, u32[]{:S(2)}) collective-permute-start(f32[9,4,1152]{2,1,0:T(4,128)S(1)} %constant_dynamic-update-slice_fusion.lists), channel_id=1, source_target_pairs={{0,56},{8,16},{16,8},{24,32},{32,24},{40,48},{48,40},{56,0},{1,57}... | collective-permute-start | bytes 497672 | tf_op jit(solution)/shard_map/ppermute | solution.py:300
  24.8 5.5 %collective-permute-start.4 = (f32[9,4,1152]{2,1,0:T(4,128)S(1)}, f32[9,4,1152]{2,1,0:T(4,128)S(1)}, u32[]{:S(2)}, u32[]{:S(2)}) collective-permute-start(f32[9,4,1152]{2,1,0:T(4,128)S(1)} %constant_dynamic-update-slice_fusion.lists), channel_id=1, source_target_pairs={{0,8},{8,0},{16,24},{24,16},{32,40},{40,32},{48,56},{56,48},{1,9},... | collective-permute-start | bytes 497672 | tf_op jit(solution)/shard_map/ppermute | solution.py:300
where the time goes:
time: 39.3 us; the launch traced here: 38.9 us
  starting transfers between devices  14.2 us (36%)
  Pallas kernels  14 us (36%)
  waiting for transfers between devices  9.18 us (23%)
  between operations  1.48 us (4%)
    ppermute x6, starting transfers between devices, swaps(): return (lax.ppermute(block, axis, first), lax.ppermute(other, axis, second))  14.2 us
    ppermute x6, waiting for transfers between devices, swaps(): return (lax.ppermute(block, axis, first), lax.ppermute(other, axis, second))  9.18 us
    pallas_call x1, Pallas kernels, call_finish(): pl.pallas_call(finish, out_shape=(jax.ShapeDtypeStruct((BX, BY, BZ), jnp....  8.46 us
    pallas_call x1, Pallas kernels, call_column(): pl.pallas_call(column, out_shape=pltpu.VMEM((PX, PY, PZ), jnp.float32), i...  3.74 us
    pallas_call x1, Pallas kernels, call_compact(): pl.pallas_call(compact, out_shape=(shape, shape, shape), in_specs=[pl.Blo...  1.78 us
  transfers between devices with their start and end apart: 6, of which 6 were waited for; matrix products, arithmetic and copies ran while one was open for 0% of the time, Pallas kernels for 10%

commit v1 on v0

--- a/solution.py
+++ b/solution.py
@@ -16,6 +16,7 @@
 REACH = 4
 WIDTH = A_DEV + 128
 BLOCK = 256
+SMALL = 128
 WIDE = 2 * BLOCK
 
 X0 = 5
@@ -34,8 +35,11 @@
 UNIT = math.sqrt(-EXPONENT)
 LOW_END = 2 * PAD + 5
 HIGH_START = BZ + PAD - 9
-SPAN = A_DEV + 128 + WIDE
-MERGED = 9 * A_DEV + SPAN
+HIGH_START_Y = BY + PAD - 9
+MIDDLE = BZ // 2
+SPAN = A_DEV + 256 + WIDE
+FRONT = 128
+MERGED = 9 * A_DEV + SPAN + FRONT
 ROWS = FCHUNK * FY
 
 
@@ -54,33 +58,44 @@
     return 1 - 2 * (lax.axis_index(axis) % 2)
 
 
-def compact(numbers, charges, cells, own, first, second, lists):
-    count = numbers[0]
-    slots = lax.broadcasted_iota(jnp.int32, (1, A_DEV), 1)
-    live = slots < count
+def live_atoms(numbers, charges, cells):
+    live = lax.broadcasted_iota(jnp.int32, (1, A_DEV), 1) < numbers[0]
     charge = jnp.where(live, charges[...], 0.0).astype(jnp.bfloat16).astype(jnp.float32)
-    places = jnp.concatenate([jnp.where(live, cells[i], 0) for i in range(3)], axis=0)
-    own[0:1, 0:A_DEV] = charge
-    own[1:4, 0:A_DEV] = places.astype(jnp.float32)
-    own[:, A_DEV:WIDTH] = jnp.full((4, WIDTH - A_DEV), count.astype(jnp.float32))
-    depth = places[2:3]
-    before = jnp.concatenate(
-        [
-            jnp.where(live & (depth < LOW_END), 1.0, 0.0),
-            jnp.where(live & (depth >= HIGH_START), 1.0, 0.0),
-            jnp.zeros((6, A_DEV), jnp.float32),
-        ],
-        axis=0,
-    )
-    near = before
+    places = [jnp.where(live, cells[i], 0) for i in range(3)]
+    rows = [charge] + [place.astype(jnp.float32) for place in places[:2]]
+    rows.append((places[2] - MIDDLE).astype(jnp.float32))
+    rows.append(jnp.zeros((4, A_DEV), jnp.float32))
+    return live, places, jnp.concatenate(rows, axis=0).astype(jnp.bfloat16)
+
+
+def running_sums(masks):
+    rows = [jnp.where(mask, 1.0, 0.0) for mask in masks]
+    rows.append(jnp.zeros((8 - len(masks), A_DEV), jnp.float32))
+    near = jnp.concatenate(rows, axis=0)
+    sums = near
     lanes = lax.broadcasted_iota(jnp.int32, (8, A_DEV), 1)
     shift = 1
     while shift < A_DEV:
-        before = before + jnp.where(lanes >= shift, pltpu.roll(before, shift, 1), 0.0)
+        sums = sums + jnp.where(lanes >= shift, pltpu.roll(sums, shift, 1), 0.0)
         shift *= 2
-    totals = before[:, A_DEV - 1 : A_DEV]
-    spot = jnp.where(near > 0.5, before - 1.0, -1.0)
-    steps = (jnp.max(totals).astype(jnp.int32) + BLOCK - 1) // BLOCK
+    return sums, near
+
+
+def pick(rows, spot, start, size):
+    want = iota((size, A_DEV), 0) + start.astype(jnp.float32)
+    hot = jnp.where(want == spot, 1.0, 0.0).astype(jnp.bfloat16)
+    return lax.dot_general(
+        rows, hot, (((1,), (1,)), ((), ())), preferred_element_type=jnp.float32
+    )
+
+
+def compact(numbers, charges, cells, first, second, lists):
+    live, places, rows = live_atoms(numbers, charges, cells)
+    depth = places[2]
+    sums, near = running_sums([live & (depth < LOW_END), live & (depth >= HIGH_START)])
+    totals = sums[:, A_DEV - 1 : A_DEV]
+    spot = jnp.where(near > 0.5, sums - 1.0, -1.0)
+    steps = (jnp.max(totals).astype(jnp.int32) + SMALL - 1) // SMALL
     for side in range(2):
         lists[side, :, 0:A_DEV] = jnp.zeros((4, A_DEV), jnp.float32)
         lists[side, :, A_DEV:WIDTH] = jnp.broadcast_to(
@@ -88,24 +103,11 @@
         )
 
     def window(k, _):
-        for side, base in enumerate((0, BZ // 2)):
-            rows = jnp.concatenate(
-                [
-                    charge,
-                    places[0:2].astype(jnp.float32),
-                    (places[2:3] - base).astype(jnp.float32),
-                    jnp.zeros((4, A_DEV), jnp.float32),
-                ],
-                axis=0,
-            ).astype(jnp.bfloat16)
-            want = iota((BLOCK, A_DEV), 0) + (k * BLOCK).astype(jnp.float32)
-            pick = jnp.where(want == spot[side : side + 1], 1.0, 0.0).astype(jnp.bfloat16)
-            moved = lax.dot_general(
-                rows, pick, (((1,), (1,)), ((), ())), preferred_element_type=jnp.float32
-            )
-            cols = pl.ds(pl.multiple_of(k * BLOCK, BLOCK), BLOCK)
+        cols = pl.ds(pl.multiple_of(k * SMALL, SMALL), SMALL)
+        for side in range(2):
+            moved = pick(rows, spot[side : side + 1], k * SMALL, SMALL)
             lists[side, 0:3, cols] = moved[0:3]
-            lists[side, 3:4, cols] = moved[3:4] + float(base)
+            lists[side, 3:4, cols] = moved[3:4] + float(MIDDLE)
         return 0
 
     lax.fori_loop(0, steps, window, 0)
@@ -114,25 +116,54 @@
     second[...] = lists[odd]
 
 
-def append(ref, brick, number, offset, dx, dy, dz, merged):
-    lanes = lax.broadcasted_iota(jnp.int32, (1, A_DEV), 1)
-    live = lanes < number
+def arrange(numbers, charges, cells, own):
+    live, places, rows = live_atoms(numbers, charges, cells)
+    high = live & (places[1] >= HIGH_START_Y)
+    low = live & (places[1] < LOW_END)
+    sums, near = running_sums([high, low, live])
+    totals = sums[:, A_DEV - 1 : A_DEV]
+    middle_at = totals[0:1] - 1.0
+    low_at = totals[2:3] - totals[1:2] - 1.0
+    spot = jnp.where(low, low_at + sums[1:2], middle_at + sums[2:3] - sums[0:1] - sums[1:2])
+    spot = jnp.where(high, sums[0:1] - 1.0, spot)
+    spot = jnp.where(live, spot, -1.0)
+    own[:, 0:A_DEV] = jnp.zeros((4, A_DEV), jnp.float32)
+    for row, total in enumerate((2, 0, 1, 2)):
+        own[row : row + 1, A_DEV:WIDTH] = jnp.broadcast_to(
+            totals[total : total + 1], (1, WIDTH - A_DEV)
+        )
+
+    def window(k, _):
+        cols = pl.ds(pl.multiple_of(k * BLOCK, BLOCK), BLOCK)
+        moved = pick(rows, spot, k * BLOCK, BLOCK)
+        own[0:3, cols] = moved[0:3]
+        own[3:4, cols] = moved[3:4] + float(MIDDLE)
+        return 0
+
+    lax.fori_loop(0, (numbers[0] + BLOCK - 1) // BLOCK, window, 0)
+
+
+def append(ref, brick, start, number, offset, dx, dy, dz, merged, padded):
     moved = (X0 - PAD + BX * dx, Y0 - PAD + BY * dy, BZ * dz - PAD)
-    rows = [ref[brick, 0:1, 0:A_DEV]]
+    padded[0:1, 0:A_DEV] = ref[brick, 0:1, 0:A_DEV]
     for i in range(3):
         place = ref[brick, 1 + i : 2 + i, 0:A_DEV] + jnp.float32(moved[i])
-        rows.append(jnp.where(live, place * UNIT, 0.0))
-    atoms = jnp.concatenate(rows + [jnp.zeros((4, A_DEV), jnp.float32)], axis=0)
-    atoms = jnp.concatenate([atoms, jnp.zeros((8, SPAN - A_DEV), jnp.float32)], axis=1)
-    atoms = pltpu.roll(atoms, offset % 128, 1)
-    start = pl.multiple_of(offset // 128 * 128, 128)
-    merged[:, pl.ds(start, 128)] += atoms[:, 0:128]
-    merged[:, pl.ds(start + 128, SPAN - 128)] = atoms[:, 128:SPAN]
+        padded[1 + i : 2 + i, 0:A_DEV] = place * UNIT
+    skip = start % 128
+    atoms = padded[:, pl.ds(pl.multiple_of(start - skip, 128), SPAN)]
+    lanes = lax.broadcasted_iota(jnp.int32, (8, SPAN), 1)
+    atoms = jnp.where((lanes >= skip) & (lanes < skip + number), atoms, 0.0)
+    room = offset % 128
+    back = jnp.where(room >= skip, 0, 128)
+    atoms = pltpu.roll(atoms, room - skip + back, 1)
+    base = pl.multiple_of(FRONT + offset - room - back, 128)
+    merged[:, pl.ds(base, 256)] += atoms[:, 0:256]
+    merged[:, pl.ds(base + 256, SPAN - 256)] = atoms[:, 256:SPAN]
     return offset + number
 
 
 def spread(merged, start, size, x0, nx, y0, ny, grid, rows_x, first):
-    cols = pl.ds(pl.multiple_of(start, BLOCK), size)
+    cols = pl.ds(pl.multiple_of(start + FRONT, 128), size)
     charge = merged[0:1, cols]
     xa = merged[1:2, cols]
     ya = merged[2:3, cols]
@@ -177,12 +208,17 @@
         spread(merged, wide * WIDE, BLOCK, x0, nx, y0, ny, grid, rows_x, False)
 
 
-def gather(ref, bricks, numbers, merged):
-    merged[:, 0:128] = jnp.zeros((8, 128), jnp.float32)
+def gather(ref, bricks, numbers, side, merged, padded):
+    merged[:, 0 : FRONT + 256] = jnp.zeros((8, FRONT + 256), jnp.float32)
     offset = jnp.int32(0)
     for brick, (dx, dy, dz) in bricks:
         number = numbers[brick, 0, 0].astype(jnp.int32)
-        offset = append(ref, brick, number, offset, dx, dy, dz, merged)
+        start = jnp.int32(0)
+        if side is not None:
+            low = numbers[brick, 2, 0].astype(jnp.int32)
+            start = jnp.where(side > 0, number - low, 0)
+            number = jnp.where(side > 0, low, numbers[brick, 1, 0].astype(jnp.int32))
+        offset = append(ref, brick, start, number, offset, dx, dy, dz, merged, padded)
     return offset
 
 
@@ -191,9 +227,10 @@
     return (step, 0, -step)
 
 
-def column(lists, grid, rows_x, merged, numbers, sem):
-    copy = pltpu.make_async_copy(lists.at[:, 0:1, A_DEV:WIDTH], numbers, sem)
+def column(lists, grid, rows_x, merged, padded, numbers, sem):
+    copy = pltpu.make_async_copy(lists.at[:, :, A_DEV:WIDTH], numbers, sem)
     copy.start()
+    padded[...] = jnp.zeros_like(padded)
     copy.wait()
     xs, zs = slots_of("gx"), slots_of("gz")
     for i in (1, 0, 2):
@@ -201,7 +238,9 @@
             lists,
             [(3 * i + j, (xs[i], 0, zs[j])) for j in (1, 0, 2)],
             numbers,
+            None,
             merged,
+            padded,
         )
         if i == 1:
             spread_all(merged, total, 0, PX, 0, PY, grid, rows_x, True)
@@ -211,18 +250,20 @@
 
 
 def finish(
-    near, far, own, charges, before, potential, forces, grid,
-    rows_x, fields, merged, numbers, charge, sems,
+    near, far, own, charges, cells, before, potential, forces, grid,
+    rows_x, fields, merged, padded, numbers, charge, place, sems,
 ):
     copies = [
-        pltpu.make_async_copy(near.at[:, 0:1, A_DEV:WIDTH], numbers.at[0], sems.at[0]),
-        pltpu.make_async_copy(far.at[:, 0:1, A_DEV:WIDTH], numbers.at[1], sems.at[1]),
-        pltpu.make_async_copy(own.at[:, 0:1, A_DEV:WIDTH], numbers.at[2, 0:1], sems.at[2]),
+        pltpu.make_async_copy(near.at[:, :, A_DEV:WIDTH], numbers.at[0], sems.at[0]),
+        pltpu.make_async_copy(far.at[:, :, A_DEV:WIDTH], numbers.at[1], sems.at[1]),
+        pltpu.make_async_copy(own.at[:, :, A_DEV:WIDTH], numbers.at[2, 0:1], sems.at[2]),
         pltpu.make_async_copy(charges, charge, sems.at[3]),
+        pltpu.make_async_copy(cells, place, sems.at[4]),
     ]
     for copy in copies:
         copy.start()
-    for copy in copies:
+    padded[...] = jnp.zeros_like(padded)
+    for copy in copies[:3]:
         copy.wait()
     xs, zs = slots_of("gx"), slots_of("gz")
     dy = toward("gy")
@@ -232,7 +273,9 @@
             ref,
             [(3 * m + j, (xs[m], step, zs[j])) for m in range(3) for j in range(3)],
             numbers.at[i],
+            step,
             merged,
+            padded,
         )
         y0 = pl.multiple_of(jnp.where(step > 0, 32, 0), 8)
         spread_all(merged, total, 0, PX, y0, 16, grid, rows_x, False)
@@ -241,6 +284,8 @@
     )
     copy.start()
 
+    for late in copies[3:]:
+        late.wait()
     forces[...] = jnp.zeros_like(forces)
     count = numbers[2, 0, 0, 0].astype(jnp.int32)
 
@@ -257,8 +302,8 @@
 
     def sample(start, size, fresh):
         cols = pl.ds(pl.multiple_of(start, BLOCK), size)
-        xa = own[0, 1:2, cols]
-        za = own[0, 3:4, cols] - float(PAD)
+        xa = place[0, :, cols].astype(jnp.float32)
+        za = (place[2, :, cols] - PAD).astype(jnp.float32)
         zi = iota((PZ, size), 0)
         zi = jnp.where(zi < 448.0, zi, zi - float(PZ))
         depth = jnp.where(zi == za, 1.0, 0.0).astype(jnp.bfloat16)
@@ -276,7 +321,7 @@
                 for i in range(FCHUNK):
                     hot_x = xa == float(c * FCHUNK + i)
                     sums[d] = sums[d] + jnp.where(hot_x, part[i], 0.0)
-        hot_y = iota((FY, size), 0) == own[0, 2:3, cols]
+        hot_y = iota((FY, size), 0) == place[1, :, cols].astype(jnp.float32)
         slots = lax.broadcasted_iota(jnp.int32, (1, size), 1) + start
         factor = jnp.where(slots < count, -0.5 * charge[0:1, cols], 0.0)
         for d in range(3):
@@ -309,10 +354,20 @@
     shape = pltpu.VMEM((4, WIDTH), jnp.float32)
     return pl.pallas_call(
         compact,
-        out_shape=(shape, shape, shape),
+        out_shape=(shape, shape),
         in_specs=[pl.BlockSpec(memory_space=pltpu.SMEM), VMEM, VMEM],
-        out_specs=(VMEM,) * 3,
+        out_specs=(VMEM,) * 2,
         scratch_shapes=[pltpu.VMEM((2, 4, WIDTH), jnp.float32)],
+    )(counts, charge, cells)
+
+
+def call_arrange(counts, charge, cells):
+    return pl.pallas_call(
+        arrange,
+        out_shape=pltpu.VMEM((4, WIDTH), jnp.float32),
+        in_specs=[pl.BlockSpec(memory_space=pltpu.SMEM), VMEM, VMEM],
+        out_specs=VMEM,
+        cost_estimate=pl.CostEstimate(flops=2 * 10**9, bytes_accessed=10**5, transcendentals=0),
     )(counts, charge, cells)
 
 
@@ -325,7 +380,8 @@
         scratch_shapes=[
             pltpu.VMEM((48, WIDE), jnp.float32),
             pltpu.VMEM((8, MERGED), jnp.float32),
-            pltpu.SMEM((9, 1, WIDTH - A_DEV), jnp.float32),
+            pltpu.VMEM((8, A_DEV + SPAN), jnp.float32),
+            pltpu.SMEM((9, 4, WIDTH - A_DEV), jnp.float32),
             pltpu.SemaphoreType.DMA,
         ],
         compiler_params=pltpu.CompilerParams(vmem_limit_bytes=LIMIT),
@@ -333,7 +389,7 @@
     )(atoms)
 
 
-def call_finish(near, far, own, charge, grid):
+def call_finish(near, far, own, charge, cells, grid):
     potential, forces, _ = pl.pallas_call(
         finish,
         out_shape=(
@@ -341,33 +397,37 @@
             jax.ShapeDtypeStruct((3, 1, A_DEV), jnp.float32),
             pltpu.VMEM((PX, PY, PZ), jnp.float32),
         ),
-        in_specs=[VMEM, VMEM, VMEM, HBM, VMEM],
+        in_specs=[VMEM, VMEM, VMEM, HBM, HBM, VMEM],
         out_specs=(HBM, VMEM, VMEM),
-        input_output_aliases={4: 2},
+        input_output_aliases={5: 2},
         scratch_shapes=[
             pltpu.VMEM((48, WIDE), jnp.float32),
             pltpu.VMEM((3, FX * FY, PZ), jnp.bfloat16),
             pltpu.VMEM((8, MERGED), jnp.float32),
-            pltpu.SMEM((3, 9, 1, WIDTH - A_DEV), jnp.float32),
+            pltpu.VMEM((8, A_DEV + SPAN), jnp.float32),
+            pltpu.SMEM((3, 9, 4, WIDTH - A_DEV), jnp.float32),
             pltpu.VMEM((1, A_DEV), jnp.float32),
-            pltpu.SemaphoreType.DMA((4,)),
+            pltpu.VMEM((3, 1, A_DEV), jnp.int32),
+            pltpu.SemaphoreType.DMA((5,)),
         ],
         compiler_params=pltpu.CompilerParams(vmem_limit_bytes=LIMIT),
-    )(near, far, own, charge, grid)
+    )(near, far, own, charge, cells, grid)
     return potential, forces
 
 
 def local(charges, cells, counts):
     charge = charges.reshape(1, A_DEV)
-    own, first, second = call_compact(counts.reshape(1), charge, cells.reshape(3, 1, A_DEV))
-    own = own[None]
+    cells = cells.reshape(3, 1, A_DEV)
+    counts = counts.reshape(1)
+    first, second = call_compact(counts, charge, cells)
+    own = call_arrange(counts, charge, cells)[None]
     first, second = swaps(first[None], second[None], "gz")
     atoms = jnp.concatenate([first, own, second], axis=0)
     first, second = swaps(atoms, atoms, "gx")
     atoms = jnp.concatenate([first, atoms, second], axis=0)
     first, second = swaps(atoms, atoms, "gy")
     grid = call_column(atoms)
-    potential, forces = call_finish(first, second, own, charge, grid)
+    potential, forces = call_finish(first, second, own, charge, cells, grid)
     return potential, forces.reshape(1, 1, 1, 3, A_DEV)
 
 

time: 39.3 us -> 38.4 us (0.977)
  waiting for transfers between devices: 9.18 us -> 7.31 us
  Pallas kernels: 14 us -> 15 us
    ppermute x6, waiting for transfers between devices: 9.18 us -> 7.31 us  [swaps(): return (lax.ppermute(block, axis, first), lax.ppermute(other, axis, second))]
    pallas_call x1 -> x2, Pallas kernels: 1.78 us -> 3.24 us  [the longest x1 1.64 us: call_compact(): pl.pallas_call(compact, out_shape=(shape, shape), in_specs=[pl.BlockSpec(...]
    pallas_call x1, Pallas kernels: 8.46 us -> 7.8 us  [call_finish(): pl.pallas_call(finish, out_shape=(jax.ShapeDtypeStruct((BX, BY, BZ), jnp....]
  transfers between devices with their start and end apart: 6 -> 6, of which waited for: 6 -> 5; matrix products, arithmetic and copies ran while one was open for 0% -> 0% of each run, Pallas kernels for 10% -> 15%
where the time goes in v1:
time: 38.4 us; the launch traced here: 38.1 us
  Pallas kernels  15 us (39%)
  starting transfers between devices  14.2 us (37%)
  waiting for transfers between devices  7.31 us (19%)
  between operations  1.49 us (4%)
    ppermute x6, starting transfers between devices, swaps(): return (lax.ppermute(block, axis, first), lax.ppermute(other, axis, second))  14.2 us
    pallas_call x1, Pallas kernels, call_finish(): pl.pallas_call(finish, out_shape=(jax.ShapeDtypeStruct((BX, BY, BZ), jnp....  7.8 us
    ppermute x6, waiting for transfers between devices, swaps(): return (lax.ppermute(block, axis, first), lax.ppermute(other, axis, second))  7.31 us
    pallas_call x1, Pallas kernels, call_column(): pl.pallas_call(column, out_shape=pltpu.VMEM((PX, PY, PZ), jnp.float32), i...  4 us
    pallas_call x1, Pallas kernels, call_compact(): pl.pallas_call(compact, out_shape=(shape, shape), in_specs=[pl.BlockSpec(...  1.64 us
    pallas_call x1, Pallas kernels, call_arrange(): pl.pallas_call(arrange, out_shape=pltpu.VMEM((4, WIDTH), jnp.float32), in...  1.6 us
  transfers between devices with their start and end apart: 6, of which 5 were waited for; matrix products, arithmetic and copies ran while one was open for 0% of the time, Pallas kernels for 15%

profile of v1, /device:TPU:1, one launch (start us, length us, event | category | flops | bytes accessed | tf_op | source)
XLA Modules:
  0.0 38.1 jit_solution(10525213319556579092)
XLA Ops:
  1.3 1.6 %shard_map.50 = (f32[4,1152]{1,0:T(4,128)S(1)}, f32[4,1152]{1,0:T(4,128)S(1)}) custom-call(s32[1]{0:T(128)} %bitcast.10.numbers, f32[1,1024]{1,0:T(1,128)} %bitcast.17, s32[3,1,1024]{2,1,0:T(1,128)} %bitcast.14), custom_call_target="tpu_custom_call" | custom-call | tf_op jit(solution)/shard_map/pallas_call | solution.py:355
  2.9 6.1 %collective-permute-start.1 = (f32[1,4,1152]{2,1,0:T(4,128)S(1)}, f32[1,4,1152]{2,1,0:T(4,128)S(1)}, u32[]{:S(2)}, u32[]{:S(2)}) collective-permute-start(f32[1,4,1152]{2,1,0:T(4,128)S(1)} %bitcast.21), channel_id=1, source_target_pairs={{0,7},{1,2},{2,1},{3,4},{4,3},{5,6},{6,5},{7,0},{8,15},{9,10},{10,... | collective-permute-start | bytes 55304 | tf_op jit(solution)/shard_map/ppermute | solution.py:345
  9.0 0.0 collective-permute-start
  9.0 1.6 %shard_map.51 = f32[4,1152]{1,0:T(4,128)S(1)} custom-call(s32[1]{0:T(128)} %bitcast.11.numbers, f32[1,1024]{1,0:T(1,128)} %bitcast.18, s32[3,1,1024]{2,1,0:T(1,128)} %bitcast.15), custom_call_target="tpu_custom_call" | custom-call | flops 2000000000 | bytes 100000 | tf_op jit(solution)/shard_map/pallas_call | solution.py:365
  10.6 0.0 collective-permute-done.1
  10.6 2.6 %collective-permute-done = f32[1,4,1152]{2,1,0:T(4,128)S(1)} collective-permute-done((f32[1,4,1152]{2,1,0:T(4,128)S(1)}, f32[1,4,1152]{2,1,0:T(4,128)S(1)}, u32[]{:S(2)}, u32[]{:S(2)}) %collective-permute-start) | collective-permute-done | bytes 18464 | tf_op jit(solution)/shard_map/ppermute | solution.py:345
  13.2 2.1 %collective-permute-start.2 = (f32[3,4,1152]{2,1,0:T(4,128)S(1)}, f32[3,4,1152]{2,1,0:T(4,128)S(1)}, u32[]{:S(2)}, u32[]{:S(2)}) collective-permute-start(f32[3,4,1152]{2,1,0:T(4,128)S(1)} %pad_maximum_fusion), channel_id=1, source_target_pairs={{0,64},{64,0},{128,192},{192,128},{1,65},{65,1},{129,193},{193,129... | collective-permute-start | bytes 165896 | tf_op jit(solution)/shard_map/ppermute | solution.py:345
  15.3 0.3 collective-permute-start.3
  15.6 0.6 %collective-permute-done.2 = f32[3,4,1152]{2,1,0:T(4,128)S(1)} collective-permute-done((f32[3,4,1152]{2,1,0:T(4,128)S(1)}, f32[3,4,1152]{2,1,0:T(4,128)S(1)}, u32[]{:S(2)}, u32[]{:S(2)}) %collective-permute-start.2) | collective-permute-done | bytes 55328 | tf_op jit(solution)/shard_map/ppermute | solution.py:345
  16.2 2.7 %collective-permute-done.3 = f32[3,4,1152]{2,1,0:T(4,128)S(1)} collective-permute-done((f32[3,4,1152]{2,1,0:T(4,128)S(1)}, f32[3,4,1152]{2,1,0:T(4,128)S(1)}, u32[]{:S(2)}, u32[]{:S(2)}) %collective-permute-start.3) | collective-permute-done | bytes 55328 | tf_op jit(solution)/shard_map/ppermute | solution.py:345
  18.9 0.0 copy-start
  18.9 0.0 copy-start.1
  18.9 5.7 %collective-permute-start.5 = (f32[9,4,1152]{2,1,0:T(4,128)S(1)}, f32[9,4,1152]{2,1,0:T(4,128)S(1)}, u32[]{:S(2)}, u32[]{:S(2)}) collective-permute-start(f32[9,4,1152]{2,1,0:T(4,128)S(1)} %constant_dynamic-update-slice_fusion.lists), channel_id=1, source_target_pairs={{0,56},{8,16},{16,8},{24,32},{32,24},{40,48},{48,40},{56,0},{1,57}... | collective-permute-start | bytes 497672 | tf_op jit(solution)/shard_map/ppermute | solution.py:345
  24.6 0.0 collective-permute-start.4
  24.6 4.0 %shard_map.52.before = f32[42,48,512]{2,1,0:T(8,128)S(1)} custom-call(f32[9,4,1152]{2,1,0:T(4,128)S(1)} %constant_dynamic-update-slice_fusion.lists), custom_call_target="tpu_custom_call" | custom-call | flops 6000000000 | bytes 1000000 | tf_op jit(solution)/shard_map/pallas_call | solution.py:375
  28.6 0.5 %collective-permute-done.5.far = f32[9,4,1152]{2,1,0:T(4,128)S(1)} collective-permute-done((f32[9,4,1152]{2,1,0:T(4,128)S(1)}, f32[9,4,1152]{2,1,0:T(4,128)S(1)}, u32[]{:S(2)}, u32[]{:S(2)}) %collective-permute-start.5) | collective-permute-done | bytes 165920 | tf_op jit(solution)/shard_map/ppermute | solution.py:345
  29.1 1.0 %collective-permute-done.4.near = f32[9,4,1152]{2,1,0:T(4,128)S(1)} collective-permute-done((f32[9,4,1152]{2,1,0:T(4,128)S(1)}, f32[9,4,1152]{2,1,0:T(4,128)S(1)}, u32[]{:S(2)}, u32[]{:S(2)}) %collective-permute-start.4) | collective-permute-done | bytes 165920 | tf_op jit(solution)/shard_map/ppermute | solution.py:345
  30.1 0.0 copy-done
  30.1 0.0 copy-done.1
  30.1 7.8 %shard_map.53 = (f32[32,32,384]{2,1,0:T(8,128)}, f32[3,1,1024]{2,1,0:T(1,128)}, f32[42,48,512]{2,1,0:T(8,128)S(1)}) custom-call(f32[9,4,1152]{2,1,0:T(4,128)S(1)} %collective-permute-done.4.near, f32[9,4,1152]{2,1,0:T(4,128)S(1)} %collective-permute-done.5.far, f32[1,4,1152]{2,1,0:T(4,128)S(1)} %bitcast.13, ...), custom_call_target="tpu_custom_call", output_to_operand_aliasing={{2}: (5, {})} | custom-call | tf_op jit(solution)/shard_map/pallas_call | solution.py:393
  (6 shorter events, 0.1 us)
Async XLA Ops:
  2.9 7.7 %collective-permute-start.1 = (f32[1,4,1152]{2,1,0:T(4,128)S(1)}, f32[1,4,1152]{2,1,0:T(4,128)S(1)}, u32[]{:S(2)}, u32[]{:S(2)}) collective-permute-start(f32[1,4,1152]{2,1,0:T(4,128)S(1)} %bitcast.21), channel_id=1, source_target_pairs={{0,7},{1,2},{2,1},{3,4},{4,3},{5,6},{6,5},{7,0},{8,15},{9,10},{10,... | collective-permute-start | bytes 55304 | tf_op jit(solution)/shard_map/ppermute | solution.py:345
  9.0 4.2 %collective-permute-start = (f32[1,4,1152]{2,1,0:T(4,128)S(1)}, f32[1,4,1152]{2,1,0:T(4,128)S(1)}, u32[]{:S(2)}, u32[]{:S(2)}) collective-permute-start(f32[1,4,1152]{2,1,0:T(4,128)S(1)} %bitcast.20), channel_id=1, source_target_pairs={{0,1},{1,0},{2,3},{3,2},{4,5},{5,4},{6,7},{7,6},{8,9},{9,8},{10,11... | collective-permute-start | bytes 55304 | tf_op jit(solution)/shard_map/ppermute | solution.py:345
  13.2 3.0 %collective-permute-start.2 = (f32[3,4,1152]{2,1,0:T(4,128)S(1)}, f32[3,4,1152]{2,1,0:T(4,128)S(1)}, u32[]{:S(2)}, u32[]{:S(2)}) collective-permute-start(f32[3,4,1152]{2,1,0:T(4,128)S(1)} %pad_maximum_fusion), channel_id=1, source_target_pairs={{0,64},{64,0},{128,192},{192,128},{1,65},{65,1},{129,193},{193,129... | collective-permute-start | bytes 165896 | tf_op jit(solution)/shard_map/ppermute | solution.py:345
  15.3 3.6 %collective-permute-start.3 = (f32[3,4,1152]{2,1,0:T(4,128)S(1)}, f32[3,4,1152]{2,1,0:T(4,128)S(1)}, u32[]{:S(2)}, u32[]{:S(2)}) collective-permute-start(f32[3,4,1152]{2,1,0:T(4,128)S(1)} %pad_maximum_fusion), channel_id=1, source_target_pairs={{0,192},{64,128},{128,64},{192,0},{1,193},{65,129},{129,65},{193,1... | collective-permute-start | bytes 165896 | tf_op jit(solution)/shard_map/ppermute | solution.py:345
  18.9 11.2 %copy-start = (s32[1,1,1,3,1024]{4,2,3,1,0:T(1,128)S(1)}, s32[1,1,1,3,1024]{4,2,3,1,0:T(1,128)}, u32[]{:S(2)}) copy-start(s32[1,1,1,3,1024]{4,2,3,1,0:T(1,128)} %param.4) | copy-start | bytes 36868
  18.9 11.2 %copy-start.1 = (f32[1,1,1,1024]{3,2,1,0:T(1,128)S(1)}, f32[1,1,1,1024]{3,2,1,0:T(1,128)}, u32[]{:S(2)}) copy-start(f32[1,1,1,1024]{3,2,1,0:T(1,128)} %param.3) | copy-start | bytes 12292
  18.9 10.2 %collective-permute-start.5 = (f32[9,4,1152]{2,1,0:T(4,128)S(1)}, f32[9,4,1152]{2,1,0:T(4,128)S(1)}, u32[]{:S(2)}, u32[]{:S(2)}) collective-permute-start(f32[9,4,1152]{2,1,0:T(4,128)S(1)} %constant_dynamic-update-slice_fusion.lists), channel_id=1, source_target_pairs={{0,56},{8,16},{16,8},{24,32},{32,24},{40,48},{48,40},{56,0},{1,57}... | collective-permute-start | bytes 497672 | tf_op jit(solution)/shard_map/ppermute | solution.py:345
  24.6 5.5 %collective-permute-start.4 = (f32[9,4,1152]{2,1,0:T(4,128)S(1)}, f32[9,4,1152]{2,1,0:T(4,128)S(1)}, u32[]{:S(2)}, u32[]{:S(2)}) collective-permute-start(f32[9,4,1152]{2,1,0:T(4,128)S(1)} %constant_dynamic-update-slice_fusion.lists), channel_id=1, source_target_pairs={{0,8},{8,0},{16,24},{24,16},{32,40},{40,32},{48,56},{56,48},{1,9},... | collective-permute-start | bytes 497672 | tf_op jit(solution)/shard_map/ppermute | solution.py:345

commit v2 on v1

--- a/solution.py
+++ b/solution.py
@@ -208,16 +208,20 @@
         spread(merged, wide * WIDE, BLOCK, x0, nx, y0, ny, grid, rows_x, False)
 
 
-def gather(ref, bricks, numbers, side, merged, padded):
+def number_of(ref, brick, row):
+    return ref[brick, row : row + 1, A_DEV:WIDTH][0, 0].astype(jnp.int32)
+
+
+def gather(ref, bricks, side, merged, padded):
     merged[:, 0 : FRONT + 256] = jnp.zeros((8, FRONT + 256), jnp.float32)
     offset = jnp.int32(0)
     for brick, (dx, dy, dz) in bricks:
-        number = numbers[brick, 0, 0].astype(jnp.int32)
+        number = number_of(ref, brick, 0)
         start = jnp.int32(0)
         if side is not None:
-            low = numbers[brick, 2, 0].astype(jnp.int32)
+            low = number_of(ref, brick, 2)
             start = jnp.where(side > 0, number - low, 0)
-            number = jnp.where(side > 0, low, numbers[brick, 1, 0].astype(jnp.int32))
+            number = jnp.where(side > 0, low, number_of(ref, brick, 1))
         offset = append(ref, brick, start, number, offset, dx, dy, dz, merged, padded)
     return offset
 
@@ -227,17 +231,13 @@
     return (step, 0, -step)
 
 
-def column(lists, grid, rows_x, merged, padded, numbers, sem):
-    copy = pltpu.make_async_copy(lists.at[:, :, A_DEV:WIDTH], numbers, sem)
-    copy.start()
+def column(lists, grid, rows_x, merged, padded):
     padded[...] = jnp.zeros_like(padded)
-    copy.wait()
     xs, zs = slots_of("gx"), slots_of("gz")
     for i in (1, 0, 2):
         total = gather(
             lists,
             [(3 * i + j, (xs[i], 0, zs[j])) for j in (1, 0, 2)],
-            numbers,
             None,
             merged,
             padded,
@@ -249,45 +249,45 @@
             spread_all(merged, total, x0, 14, 0, PY, grid, rows_x, False)
 
 
+def slab(turn, lists, grid, rows_x, merged, padded):
+    padded[...] = jnp.zeros_like(padded)
+    xs, zs = slots_of("gx"), slots_of("gz")
+    dy = toward("gy") * turn
+    total = gather(
+        lists,
+        [(3 * m + j, (xs[m], dy, zs[j])) for m in range(3) for j in range(3)],
+        dy,
+        merged,
+        padded,
+    )
+    y0 = pl.multiple_of(jnp.where(dy > 0, 32, 0), 8)
+    spread_all(merged, total, 0, PX, y0, 16, grid, rows_x, False)
+
+
+def add_slab(turn, lists, before, grid, rows_x, merged, padded):
+    slab(turn, lists, grid, rows_x, merged, padded)
+
+
 def finish(
-    near, far, own, charges, cells, before, potential, forces, grid,
-    rows_x, fields, merged, padded, numbers, charge, place, sems,
+    lists, own, charges, cells, before, potential, forces, grid,
+    rows_x, fields, merged, padded, charge, place, sems,
 ):
-    copies = [
-        pltpu.make_async_copy(near.at[:, :, A_DEV:WIDTH], numbers.at[0], sems.at[0]),
-        pltpu.make_async_copy(far.at[:, :, A_DEV:WIDTH], numbers.at[1], sems.at[1]),
-        pltpu.make_async_copy(own.at[:, :, A_DEV:WIDTH], numbers.at[2, 0:1], sems.at[2]),
-        pltpu.make_async_copy(charges, charge, sems.at[3]),
-        pltpu.make_async_copy(cells, place, sems.at[4]),
+    late = [
+        pltpu.make_async_copy(charges, charge, sems.at[1]),
+        pltpu.make_async_copy(cells, place, sems.at[2]),
     ]
-    for copy in copies:
+    for copy in late:
         copy.start()
-    padded[...] = jnp.zeros_like(padded)
-    for copy in copies[:3]:
-        copy.wait()
-    xs, zs = slots_of("gx"), slots_of("gz")
-    dy = toward("gy")
-    for i, ref in enumerate((near, far)):
-        step = dy * (1 - 2 * i)
-        total = gather(
-            ref,
-            [(3 * m + j, (xs[m], step, zs[j])) for m in range(3) for j in range(3)],
-            numbers.at[i],
-            step,
-            merged,
-            padded,
-        )
-        y0 = pl.multiple_of(jnp.where(step > 0, 32, 0), 8)
-        spread_all(merged, total, 0, PX, y0, 16, grid, rows_x, False)
+    slab(1, lists, grid, rows_x, merged, padded)
     copy = pltpu.make_async_copy(
         grid.at[X0 : X0 + BX, Y0 : Y0 + BY, 0:BZ], potential, sems.at[0]
     )
     copy.start()
 
-    for late in copies[3:]:
-        late.wait()
+    for one in late:
+        one.wait()
     forces[...] = jnp.zeros_like(forces)
-    count = numbers[2, 0, 0, 0].astype(jnp.int32)
+    count = number_of(own, 0, 0)
 
     def build(c):
         gx, gy, gz = [], [], []
@@ -381,15 +381,30 @@
             pltpu.VMEM((48, WIDE), jnp.float32),
             pltpu.VMEM((8, MERGED), jnp.float32),
             pltpu.VMEM((8, A_DEV + SPAN), jnp.float32),
-            pltpu.SMEM((9, 4, WIDTH - A_DEV), jnp.float32),
-            pltpu.SemaphoreType.DMA,
         ],
         compiler_params=pltpu.CompilerParams(vmem_limit_bytes=LIMIT),
         cost_estimate=pl.CostEstimate(flops=6 * 10**9, bytes_accessed=10**6, transcendentals=0),
     )(atoms)
 
 
-def call_finish(near, far, own, charge, cells, grid):
+def call_slab(turn, lists, grid):
+    return pl.pallas_call(
+        functools.partial(add_slab, turn),
+        out_shape=pltpu.VMEM((PX, PY, PZ), jnp.float32),
+        in_specs=[VMEM, VMEM],
+        out_specs=VMEM,
+        input_output_aliases={1: 0},
+        scratch_shapes=[
+            pltpu.VMEM((48, WIDE), jnp.float32),
+            pltpu.VMEM((8, MERGED), jnp.float32),
+            pltpu.VMEM((8, A_DEV + SPAN), jnp.float32),
+        ],
+        compiler_params=pltpu.CompilerParams(vmem_limit_bytes=LIMIT),
+        cost_estimate=pl.CostEstimate(flops=10**9, bytes_accessed=10**6, transcendentals=0),
+    )(lists, grid)
+
+
+def call_finish(lists, own, charge, cells, grid):
     potential, forces, _ = pl.pallas_call(
         finish,
         out_shape=(
@@ -397,21 +412,20 @@
             jax.ShapeDtypeStruct((3, 1, A_DEV), jnp.float32),
             pltpu.VMEM((PX, PY, PZ), jnp.float32),
         ),
-        in_specs=[VMEM, VMEM, VMEM, HBM, HBM, VMEM],
+        in_specs=[VMEM, VMEM, HBM, HBM, VMEM],
         out_specs=(HBM, VMEM, VMEM),
-        input_output_aliases={5: 2},
+        input_output_aliases={4: 2},
         scratch_shapes=[
             pltpu.VMEM((48, WIDE), jnp.float32),
             pltpu.VMEM((3, FX * FY, PZ), jnp.bfloat16),
             pltpu.VMEM((8, MERGED), jnp.float32),
             pltpu.VMEM((8, A_DEV + SPAN), jnp.float32),
-            pltpu.SMEM((3, 9, 4, WIDTH - A_DEV), jnp.float32),
             pltpu.VMEM((1, A_DEV), jnp.float32),
             pltpu.VMEM((3, 1, A_DEV), jnp.int32),
-            pltpu.SemaphoreType.DMA((5,)),
+            pltpu.SemaphoreType.DMA((3,)),
         ],
         compiler_params=pltpu.CompilerParams(vmem_limit_bytes=LIMIT),
-    )(near, far, own, charge, cells, grid)
+    )(lists, own, charge, cells, grid)
     return potential, forces
 
 
@@ -427,7 +441,8 @@
     atoms = jnp.concatenate([first, atoms, second], axis=0)
     first, second = swaps(atoms, atoms, "gy")
     grid = call_column(atoms)
-    potential, forces = call_finish(first, second, own, charge, cells, grid)
+    grid = call_slab(-1, second, grid)
+    potential, forces = call_finish(first, own, charge, cells, grid)
     return potential, forces.reshape(1, 1, 1, 3, A_DEV)
 
 

time: 38.4 us -> 36.5 us (0.951)
  Pallas kernels: 15 us -> 13.6 us
  waiting for transfers between devices: 7.31 us -> 6.85 us
    pallas_call x1, Pallas kernels: 7.8 us -> 5.78 us  [call_finish(): pl.pallas_call(finish, out_shape=(jax.ShapeDtypeStruct((BX, BY, BZ), jnp....]
    pallas_call x0 -> x1, Pallas kernels: none -> 1.08 us  [call_slab(): pl.pallas_call(functools.partial(add_slab, turn), out_shape=pltpu.VMEM((P...]
    pallas_call x1, Pallas kernels: 4 us -> 3.22 us  [call_column(): pl.pallas_call(column, out_shape=pltpu.VMEM((PX, PY, PZ), jnp.float32), i...]
    ppermute x6, waiting for transfers between devices: 7.31 us -> 6.85 us  [swaps(): return (lax.ppermute(block, axis, first), lax.ppermute(other, axis, second))]
  transfers between devices with their start and end apart: 6 -> 6, of which waited for: 5 -> 4; matrix products, arithmetic and copies ran while one was open for 0% -> 0% of each run, Pallas kernels for 15% -> 17%
where the time goes in v2:
time: 36.5 us; the launch traced here: 36.2 us
  starting transfers between devices  14.2 us (39%)
  Pallas kernels  13.6 us (37%)
  waiting for transfers between devices  6.85 us (19%)
  between operations  1.52 us (4%)
    ppermute x6, starting transfers between devices, swaps(): return (lax.ppermute(block, axis, first), lax.ppermute(other, axis, second))  14.2 us
    ppermute x6, waiting for transfers between devices, swaps(): return (lax.ppermute(block, axis, first), lax.ppermute(other, axis, second))  6.85 us
    pallas_call x1, Pallas kernels, call_finish(): pl.pallas_call(finish, out_shape=(jax.ShapeDtypeStruct((BX, BY, BZ), jnp....  5.78 us
    pallas_call x1, Pallas kernels, call_column(): pl.pallas_call(column, out_shape=pltpu.VMEM((PX, PY, PZ), jnp.float32), i...  3.22 us
    pallas_call x1, Pallas kernels, call_arrange(): pl.pallas_call(arrange, out_shape=pltpu.VMEM((4, WIDTH), jnp.float32), in...  1.87 us
    pallas_call x1, Pallas kernels, call_compact(): pl.pallas_call(compact, out_shape=(shape, shape), in_specs=[pl.BlockSpec(...  1.64 us
    pallas_call x1, Pallas kernels, call_slab(): pl.pallas_call(functools.partial(add_slab, turn), out_shape=pltpu.VMEM((P...  1.08 us
  transfers between devices with their start and end apart: 6, of which 4 were waited for; matrix products, arithmetic and copies ran while one was open for 0% of the time, Pallas kernels for 17%

profile of v2, /device:TPU:1, one launch (start us, length us, event | category | flops | bytes accessed | tf_op | source)
XLA Modules:
  0.0 36.2 jit_solution(2851764260878852281)
XLA Ops:
  1.3 1.6 %shard_map.50 = (f32[4,1152]{1,0:T(4,128)S(1)}, f32[4,1152]{1,0:T(4,128)S(1)}) custom-call(s32[1]{0:T(128)} %bitcast.10.numbers, f32[1,1024]{1,0:T(1,128)} %bitcast.17, s32[3,1,1024]{2,1,0:T(1,128)} %bitcast.14), custom_call_target="tpu_custom_call" | custom-call | tf_op jit(solution)/shard_map/pallas_call | solution.py:355
  2.9 6.1 %collective-permute-start.1 = (f32[1,4,1152]{2,1,0:T(4,128)S(1)}, f32[1,4,1152]{2,1,0:T(4,128)S(1)}, u32[]{:S(2)}, u32[]{:S(2)}) collective-permute-start(f32[1,4,1152]{2,1,0:T(4,128)S(1)} %bitcast.21), channel_id=1, source_target_pairs={{0,7},{1,2},{2,1},{3,4},{4,3},{5,6},{6,5},{7,0},{8,15},{9,10},{10,... | collective-permute-start | bytes 55304 | tf_op jit(solution)/shard_map/ppermute | solution.py:345
  9.0 0.0 collective-permute-start
  9.0 1.9 %shard_map.51 = f32[4,1152]{1,0:T(4,128)S(1)} custom-call(s32[1]{0:T(128)} %bitcast.11.numbers, f32[1,1024]{1,0:T(1,128)} %bitcast.18, s32[3,1,1024]{2,1,0:T(1,128)} %bitcast.15), custom_call_target="tpu_custom_call" | custom-call | flops 2000000000 | bytes 100000 | tf_op jit(solution)/shard_map/pallas_call | solution.py:365
  10.9 0.0 collective-permute-done.1
  10.9 2.3 %collective-permute-done = f32[1,4,1152]{2,1,0:T(4,128)S(1)} collective-permute-done((f32[1,4,1152]{2,1,0:T(4,128)S(1)}, f32[1,4,1152]{2,1,0:T(4,128)S(1)}, u32[]{:S(2)}, u32[]{:S(2)}) %collective-permute-start) | collective-permute-done | bytes 18464 | tf_op jit(solution)/shard_map/ppermute | solution.py:345
  13.2 2.1 %collective-permute-start.2 = (f32[3,4,1152]{2,1,0:T(4,128)S(1)}, f32[3,4,1152]{2,1,0:T(4,128)S(1)}, u32[]{:S(2)}, u32[]{:S(2)}) collective-permute-start(f32[3,4,1152]{2,1,0:T(4,128)S(1)} %pad_maximum_fusion), channel_id=1, source_target_pairs={{0,64},{64,0},{128,192},{192,128},{1,65},{65,1},{129,193},{193,129... | collective-permute-start | bytes 165896 | tf_op jit(solution)/shard_map/ppermute | solution.py:345
  15.3 0.3 collective-permute-start.3
  15.6 0.6 %collective-permute-done.2 = f32[3,4,1152]{2,1,0:T(4,128)S(1)} collective-permute-done((f32[3,4,1152]{2,1,0:T(4,128)S(1)}, f32[3,4,1152]{2,1,0:T(4,128)S(1)}, u32[]{:S(2)}, u32[]{:S(2)}) %collective-permute-start.2) | collective-permute-done | bytes 55328 | tf_op jit(solution)/shard_map/ppermute | solution.py:345
  16.2 2.7 %collective-permute-done.3 = f32[3,4,1152]{2,1,0:T(4,128)S(1)} collective-permute-done((f32[3,4,1152]{2,1,0:T(4,128)S(1)}, f32[3,4,1152]{2,1,0:T(4,128)S(1)}, u32[]{:S(2)}, u32[]{:S(2)}) %collective-permute-start.3) | collective-permute-done | bytes 55328 | tf_op jit(solution)/shard_map/ppermute | solution.py:345
  18.9 5.7 %collective-permute-start.5 = (f32[9,4,1152]{2,1,0:T(4,128)S(1)}, f32[9,4,1152]{2,1,0:T(4,128)S(1)}, u32[]{:S(2)}, u32[]{:S(2)}) collective-permute-start(f32[9,4,1152]{2,1,0:T(4,128)S(1)} %constant_dynamic-update-slice_fusion.lists), channel_id=1, source_target_pairs={{0,56},{8,16},{16,8},{24,32},{32,24},{40,48},{48,40},{56,0},{1,57}... | collective-permute-start | bytes 497672 | tf_op jit(solution)/shard_map/ppermute | solution.py:345
  24.6 0.0 collective-permute-start.4
  24.6 3.2 %shard_map.52.before = f32[42,48,512]{2,1,0:T(8,128)S(1)} custom-call(f32[9,4,1152]{2,1,0:T(4,128)S(1)} %constant_dynamic-update-slice_fusion.lists), custom_call_target="tpu_custom_call" | custom-call | flops 6000000000 | bytes 1000000 | tf_op jit(solution)/shard_map/pallas_call | solution.py:375
  27.8 0.0 copy-start
  27.8 0.0 copy-start.1
  27.8 1.3 %collective-permute-done.5.lists = f32[9,4,1152]{2,1,0:T(4,128)S(1)} collective-permute-done((f32[9,4,1152]{2,1,0:T(4,128)S(1)}, f32[9,4,1152]{2,1,0:T(4,128)S(1)}, u32[]{:S(2)}, u32[]{:S(2)}) %collective-permute-start.5) | collective-permute-done | bytes 165920 | tf_op jit(solution)/shard_map/ppermute | solution.py:345
  29.1 1.1 %shard_map.53.before = f32[42,48,512]{2,1,0:T(8,128)S(1)} custom-call(f32[9,4,1152]{2,1,0:T(4,128)S(1)} %collective-permute-done.5.lists, f32[42,48,512]{2,1,0:T(8,128)S(1)} %shard_map.52.before), custom_call_target="tpu_custom_call", output_to_operand_aliasing={{}: (1, {})} | custom-call | flops 1000000000 | bytes 1000000 | tf_op jit(solution)/shard_map/pallas_call | solution.py:391
  30.2 0.0 collective-permute-done.4.lists
  30.2 0.0 copy-done
  30.2 0.0 copy-done.1
  30.2 5.8 %shard_map.54 = (f32[32,32,384]{2,1,0:T(8,128)}, f32[3,1,1024]{2,1,0:T(1,128)}, f32[42,48,512]{2,1,0:T(8,128)S(1)}) custom-call(f32[9,4,1152]{2,1,0:T(4,128)S(1)} %collective-permute-done.4.lists, f32[1,4,1152]{2,1,0:T(4,128)S(1)} %bitcast.13, f32[1,1024]{1,0:T(1,128)S(1)} %bitcast.19, s32[3,1,1024]{2,1,0:T(1,128)S(1)} %bitcast.16, ...), custom_call_target="tpu_custom_call", output_to_operand_aliasing={{2}: (4, {})} | custom-call | tf_op jit(solution)/shard_map/pallas_call | solution.py:408
  (6 shorter events, 0.1 us)
Async XLA Ops:
  2.9 8.0 %collective-permute-start.1 = (f32[1,4,1152]{2,1,0:T(4,128)S(1)}, f32[1,4,1152]{2,1,0:T(4,128)S(1)}, u32[]{:S(2)}, u32[]{:S(2)}) collective-permute-start(f32[1,4,1152]{2,1,0:T(4,128)S(1)} %bitcast.21), channel_id=1, source_target_pairs={{0,7},{1,2},{2,1},{3,4},{4,3},{5,6},{6,5},{7,0},{8,15},{9,10},{10,... | collective-permute-start | bytes 55304 | tf_op jit(solution)/shard_map/ppermute | solution.py:345
  9.0 4.2 %collective-permute-start = (f32[1,4,1152]{2,1,0:T(4,128)S(1)}, f32[1,4,1152]{2,1,0:T(4,128)S(1)}, u32[]{:S(2)}, u32[]{:S(2)}) collective-permute-start(f32[1,4,1152]{2,1,0:T(4,128)S(1)} %bitcast.20), channel_id=1, source_target_pairs={{0,1},{1,0},{2,3},{3,2},{4,5},{5,4},{6,7},{7,6},{8,9},{9,8},{10,11... | collective-permute-start | bytes 55304 | tf_op jit(solution)/shard_map/ppermute | solution.py:345
  13.2 3.0 %collective-permute-start.2 = (f32[3,4,1152]{2,1,0:T(4,128)S(1)}, f32[3,4,1152]{2,1,0:T(4,128)S(1)}, u32[]{:S(2)}, u32[]{:S(2)}) collective-permute-start(f32[3,4,1152]{2,1,0:T(4,128)S(1)} %pad_maximum_fusion), channel_id=1, source_target_pairs={{0,64},{64,0},{128,192},{192,128},{1,65},{65,1},{129,193},{193,129... | collective-permute-start | bytes 165896 | tf_op jit(solution)/shard_map/ppermute | solution.py:345
  15.3 3.6 %collective-permute-start.3 = (f32[3,4,1152]{2,1,0:T(4,128)S(1)}, f32[3,4,1152]{2,1,0:T(4,128)S(1)}, u32[]{:S(2)}, u32[]{:S(2)}) collective-permute-start(f32[3,4,1152]{2,1,0:T(4,128)S(1)} %pad_maximum_fusion), channel_id=1, source_target_pairs={{0,192},{64,128},{128,64},{192,0},{1,193},{65,129},{129,65},{193,1... | collective-permute-start | bytes 165896 | tf_op jit(solution)/shard_map/ppermute | solution.py:345
  18.9 10.2 %collective-permute-start.5 = (f32[9,4,1152]{2,1,0:T(4,128)S(1)}, f32[9,4,1152]{2,1,0:T(4,128)S(1)}, u32[]{:S(2)}, u32[]{:S(2)}) collective-permute-start(f32[9,4,1152]{2,1,0:T(4,128)S(1)} %constant_dynamic-update-slice_fusion.lists), channel_id=1, source_target_pairs={{0,56},{8,16},{16,8},{24,32},{32,24},{40,48},{48,40},{56,0},{1,57}... | collective-permute-start | bytes 497672 | tf_op jit(solution)/shard_map/ppermute | solution.py:345
  24.6 5.6 %collective-permute-start.4 = (f32[9,4,1152]{2,1,0:T(4,128)S(1)}, f32[9,4,1152]{2,1,0:T(4,128)S(1)}, u32[]{:S(2)}, u32[]{:S(2)}) collective-permute-start(f32[9,4,1152]{2,1,0:T(4,128)S(1)} %constant_dynamic-update-slice_fusion.lists), channel_id=1, source_target_pairs={{0,8},{8,0},{16,24},{24,16},{32,40},{40,32},{48,56},{56,48},{1,9},... | collective-permute-start | bytes 497672 | tf_op jit(solution)/shard_map/ppermute | solution.py:345
  27.8 2.4 %copy-start = (s32[1,1,1,3,1024]{4,2,3,1,0:T(1,128)S(1)}, s32[1,1,1,3,1024]{4,2,3,1,0:T(1,128)}, u32[]{:S(2)}) copy-start(s32[1,1,1,3,1024]{4,2,3,1,0:T(1,128)} %param.4) | copy-start | bytes 36868
  27.8 2.4 %copy-start.1 = (f32[1,1,1,1024]{3,2,1,0:T(1,128)S(1)}, f32[1,1,1,1024]{3,2,1,0:T(1,128)}, u32[]{:S(2)}) copy-start(f32[1,1,1,1024]{3,2,1,0:T(1,128)} %param.3) | copy-start | bytes 12292
